TPU v7x, 128 devices: a whole 4x4x4 slice. The times are simulated.
128 devices in a mesh: face: 4 (over z_hi, core), tile: 32 (over y, z_lo, x).
Axes of the slice: x: 4, y: 4, z: 4 (z_hi: 2, z_lo: 2; z = z_hi * 2 + z_lo), core: 2. Of those that a mesh axis runs over, the one named last changes fastest.
Arguments:
- state: float32 [4, 16, 3072, 768], P(None, None, ('face', 'tile')), may hold values from -6 to 6
- wave_speed: float32 [16], replicated, may hold values from 0.1 to 0.45
- seam_turns: int32 [4], replicated, may hold values from 0 to 3
- layer_mass: float32 [16], replicated, may hold values from 0.5 to 2
- link_source: int32 [128, 128, 128], P(('face', 'tile')), may hold values from 0 to 18431
- link_row: int32 [128, 128, 128], P(('face', 'tile')), may hold values from 0 to 3, as said below
- link_weight: float32 [128, 128, 128], P(('face', 'tile')), may hold values from 0.1 to 1
- link_count: int32 [128, 128], P(('face', 'tile')), may hold values from 42 to 128, as said below
Outputs:
- new_state: float32 [4, 16, 3072, 768], P(None, None, ('face', 'tile'))
- zonal_means: float32 [512, 64], P(('face', 'tile'))
- streamfunction: float32 [512, 16], P(('face', 'tile'))
Inputs may be any that keep to these rules, and one draw needn't show every extreme that they name: `link_row`: slot j below 4 of every tile and band holds row j. `link_count`: every tile has a full count 128 to some band and every band receives a full count from some tile.
All inputs are finite; a program needn't handle non-finite values.
Results may differ from a plain program's by a relative error of at most 0.0003.
Values sent between devices are 32-bit elements; how exact they have to be, the bound alone decides.
A program may use at most 128 MiB of HBM per device.

v0:
```python
import jax
import jax.numpy as jnp
from jax import lax
from jax.experimental import pallas as pl
from jax.experimental.pallas import tpu as pltpu
from jax.sharding import PartitionSpec as P

SUBSTEPS = 4
BAND_ROWS = 4
FIELDS = 4
GROUP = 8
LANES = 128
GATHERED = 8
SCALE = 10.0**-SUBSTEPS

f32 = jnp.float32
bf16 = jnp.bfloat16


def north_of(q):
    width = q.shape[1]
    rolled = pltpu.roll(q, width - 1, 1)
    tail = rolled[:, width - LANES :]
    lane = lax.broadcasted_iota(jnp.int32, tail.shape, 1)
    tail = jnp.where(lane == LANES - 1, 0.0, tail)
    return jnp.concatenate([rolled[:, : width - LANES], tail], axis=1)


def south_of(q):
    rolled = pltpu.roll(q, 1, 1)
    head = rolled[:, :LANES]
    lane = lax.broadcasted_iota(jnp.int32, head.shape, 1)
    head = jnp.where(lane == 0, 0.0, head)
    return jnp.concatenate([head, rolled[:, LANES:]], axis=1)


def turned(wind, turn):
    cosine, sine = turn
    east, north = wind
    return cosine * east - sine * north, sine * east + cosine * north


def column(source, target, group, at, courant, turn_west=None, turn_east=None):
    mid = [source[group, at, c] for c in range(FIELDS)]
    west = [source[group, at - 1, c] for c in range(FIELDS)]
    east = [source[group, at + 1, c] for c in range(FIELDS)]
    if turn_west is not None:
        west[0], west[1] = turned(west[:2], turn_west)
    if turn_east is not None:
        east[0], east[1] = turned(east[:2], turn_east)
    north = [north_of(q) for q in mid]
    south = [south_of(q) for q in mid]
    base = [
        6.0 * mid[c] + ((west[c] + east[c]) + (north[c] + south[c]))
        for c in range(FIELDS)
    ]
    spread = courant * ((east[0] - west[0]) + (north[1] - south[1]))
    push_x = courant * ((east[3] - west[3]) + (east[2] - west[2]))
    push_y = courant * ((north[3] - south[3]) + (north[2] - south[2]))
    target[group, at, 0] = base[0] - push_x
    target[group, at, 1] = base[1] - push_y
    target[group, at, 2] = base[2] - 0.25 * spread
    target[group, at, 3] = base[3] - spread


def quarter(code):
    cosine = jnp.where(code == 0, 1.0, jnp.where(code == 2, -1.0, 0.0))
    sine = jnp.where(code == 1, 1.0, jnp.where(code == 3, -1.0, 0.0))
    return cosine.astype(f32), sine.astype(f32)


def per_level(scalars, group):
    level = lax.broadcasted_iota(jnp.int32, (GROUP, LANES), 0)
    out = jnp.zeros((GROUP, LANES), f32)
    for k in range(GROUP):
        out = jnp.where(level == k, scalars[group * GROUP + k], out)
    return out


def split(value):
    high = value.astype(bf16)
    return high, (value - high.astype(f32)).astype(bf16)


def kernel(
    n_face, n_tile, cols, halo,
    wave, turns, mass, counts, state, source, row, weight,
    new_state, zonal, stream,
    first, odd, even, slab, cells, picked, courants, masses, rows, weights,
    spots0, spots1, sums, inbox,
    load_sem, row_sem, weight_sem, store_sem, spot_sem, send_sem, recv_sem,
    out_sem, in_sem,
):
    face, tile = lax.axis_index("face"), lax.axis_index("tile")
    devices = n_face * n_tile
    me = face * n_tile + tile
    levels = wave.shape[0]
    groups = levels // GROUP
    width = state.shape[2]
    repeat = width // LANES
    mesh_id = pl.DeviceIdType.MESH

    def place(index):
        index = lax.rem(index, devices)
        return lax.div(index, n_tile), lax.rem(index, n_tile)

    right, left = place(me + 1), place(me + devices - 1)

    def strip(ref, j):
        return ref.at[:, :, pl.ds(j * LANES, LANES)]

    loads = [
        pltpu.make_async_copy(strip(state, j), slab.at[:, j], load_sem.at[j])
        for j in range(repeat)
    ]
    for load in loads:
        load.start()
    row_load = pltpu.make_async_copy(row, rows, row_sem)
    row_load.start()
    weight_load = pltpu.make_async_copy(weight, weights, weight_sem)
    weight_load.start()

    barrier = pltpu.get_barrier_semaphore()

    def greet(i, carry):
        pl.semaphore_signal(barrier, inc=1, device_id=place(me + i), device_id_type=mesh_id)
        return carry

    lax.fori_loop(1, devices, greet, 0)

    for g in range(groups):
        courants[g] = 5.0 * per_level(wave, g)
        masses[g] = per_level(mass, g)

    def wide(value):
        return jnp.concatenate([value] * repeat, axis=1)

    def lift(g, x):
        for c in range(FIELDS):
            for j in range(repeat):
                lifted = slab[c, j, pl.ds(g * GROUP * cols + x, GROUP, stride=cols), :]
                lifted = 0.5 * lifted if c == 2 else lifted
                first[g, x + halo, c, :, pl.ds(j * LANES, LANES)] = lifted

    for load in loads:
        load.wait()

    def lift_edge(i, carry):
        g, j = lax.div(i, 2 * halo), lax.rem(i, 2 * halo)
        lift(g, j + (cols - 2 * halo) * lax.div(j, halo))
        return carry

    lax.fori_loop(0, groups * 2 * halo, lift_edge, 0)

    pl.semaphore_wait(barrier, devices - 1)

    def halo_copy(side, g):
        if side == 0:
            here, there, to = cols, 0, right
        else:
            here, there, to = halo, cols + halo, left
        return pltpu.make_async_remote_copy(
            src_ref=first.at[g, pl.ds(here, halo)],
            dst_ref=first.at[g, pl.ds(there, halo)],
            send_sem=send_sem.at[side, g],
            recv_sem=recv_sem.at[side, g],
            device_id=to,
            device_id_type=mesh_id,
        )

    for g in range(groups):
        for side in range(2):
            halo_copy(side, g).start()

    def lift_inner(i, carry):
        n = cols - 2 * halo
        lift(lax.div(i, n), halo + lax.rem(i, n))
        return carry

    lax.fori_loop(0, groups * (cols - 2 * halo), lift_inner, 0)

    steps = [(first, odd), (odd, even), (even, odd), (odd, even)]

    for s, (old, new) in enumerate(steps, 1):
        n = cols - 2 * s

        def inner(i, carry, old=old, new=new, s=s, n=n):
            g, x = lax.div(i, n), lax.rem(i, n)
            column(old, new, g, x + s + halo, wide(courants[g]))
            return carry

        lax.fori_loop(0, groups * n, inner, 0, unroll=2)

    lane = lax.broadcasted_iota(jnp.int32, (GROUP, width), 1)

    def finish(x):
        values = {}
        for g in range(groups):
            for c in range(FIELDS):
                value = even[g, x + halo, c] * (2.0 * SCALE if c == 2 else SCALE)
                for j in range(repeat):
                    part = value[:, j * LANES : (j + 1) * LANES]
                    slab[c, j, pl.ds(g * GROUP * cols + x, GROUP, stride=cols), :] = part
                values[c, g] = value
        blocks = [values[c, g] for c in range(FIELDS) for g in range(groups)]
        blocks += [values[1, g] * (wide(masses[g]) + values[3, g]) for g in range(groups)]
        blocks.append(jnp.ones((GROUP, width), f32))
        spare = LANES - GROUP * len(blocks)
        blocks.append(jnp.zeros((spare, width), f32))
        start = pl.multiple_of(x * width, width)
        cells[pl.ds(start, width), :] = jnp.concatenate(blocks, axis=0).T

    def finish_inner(i, carry):
        finish(halo + i)
        return carry

    lax.fori_loop(0, cols - 2 * halo, finish_inner, 0)

    west_cos, west_sin = quarter(jnp.where(tile == 0, turns[face], 0))
    east_cos, east_sin = quarter(jnp.where(tile == n_tile - 1, turns[lax.rem(face + 1, n_face)], 0))

    def edges(g, carry):
        courant = wide(courants[g])
        halo_copy(0, g).wait_recv()
        for s, (old, new) in enumerate(steps, 1):
            for x in range(s - halo, s):
                column(
                    old, new, g, x + halo, courant,
                    turn_west=(west_cos, west_sin) if x == 0 else None,
                    turn_east=(west_cos, -west_sin) if x == -1 else None,
                )
        halo_copy(1, g).wait_recv()
        for s, (old, new) in enumerate(steps, 1):
            for x in range(cols - s, cols + halo - s):
                column(
                    old, new, g, x + halo, courant,
                    turn_west=(east_cos, east_sin) if x == cols else None,
                    turn_east=(east_cos, -east_sin) if x == cols - 1 else None,
                )
        return carry

    for g in range(groups):
        edges(g, 0)

    def finish_edge(i, carry):
        finish(i + (cols - 2 * halo) * lax.div(i, halo))
        return carry

    lax.fori_loop(0, 2 * halo, finish_edge, 0)

    stores = [
        pltpu.make_async_copy(slab.at[:, j], strip(new_state, j), store_sem.at[j])
        for j in range(repeat)
    ]
    for store in stores:
        store.start()

    row_load.wait()
    weight_load.wait()
    spots = (spots0, spots1)
    rounds = devices // GATHERED
    slots = rows.shape[1]

    def first_band(turn):
        return pl.multiple_of(lax.rem(lax.div(me, GATHERED) + turn, rounds) * GATHERED, GATHERED)

    def spot_copy(turn, slot):
        return pltpu.make_async_copy(
            source.at[pl.ds(first_band(turn), GATHERED)], spots[slot], spot_sem.at[slot]
        )

    def pick(slot):
        for k in range(GATHERED):
            for j in range(slots):
                picked[slot, k, pl.ds(j, 1), :] = cells[pl.ds(spots[slot][k, j], 1), :]

    sub = lax.broadcasted_iota(jnp.int32, (2 * BAND_ROWS, slots), 0)
    link = lax.broadcasted_iota(jnp.int32, (2 * BAND_ROWS, slots), 1)

    def add_up(turn, slot):
        start = first_band(turn)
        for k in range(GATHERED):
            band = start + k
            w = weights[pl.ds(band, 1), :]
            high = w.astype(bf16).astype(f32)
            part = jnp.where(sub < BAND_ROWS, high, w - high)
            mine = (rows[pl.ds(band, 1), :] == lax.rem(sub, BAND_ROWS)) & (link < counts[band])
            lhs = jnp.where(mine, part, 0.0).astype(bf16)
            high_cells, low_cells = split(picked[slot, k])
            product = jnp.dot(
                lhs,
                jnp.concatenate([high_cells, low_cells], axis=1),
                preferred_element_type=f32,
            )
            sums[band] = (
                product[:BAND_ROWS, :LANES]
                + product[:BAND_ROWS, LANES:]
                + product[BAND_ROWS:, :LANES]
            )
        for k in range(GATHERED):
            band = start + k

            @pl.when(band != me)
            def _():
                pltpu.make_async_remote_copy(
                    src_ref=sums.at[band],
                    dst_ref=inbox.at[me],
                    send_sem=out_sem,
                    recv_sem=in_sem,
                    device_id=place(band),
                    device_id_type=mesh_id,
                ).start()

            @pl.when(band == me)
            def _():
                inbox[me] = sums[band]

    spot_copy(0, 0).start()
    spot_copy(1, 1).start()

    def two_rounds(i, carry):
        for slot in range(2):
            turn = 2 * i + slot
            spot_copy(turn, slot).wait()
            pick(slot)

            @pl.when(turn + 2 < rounds)
            def _():
                spot_copy(turn + 2, slot).start()

            add_up(turn, slot)
        return carry

    lax.fori_loop(0, rounds // 2, two_rounds, 0)

    others = pltpu.make_async_remote_copy(
        src_ref=sums.at[pl.ds(0, devices - 1)],
        dst_ref=inbox.at[pl.ds(0, devices - 1)],
        send_sem=out_sem,
        recv_sem=in_sem,
        device_id=right,
        device_id_type=mesh_id,
    )
    others.wait_recv()
    total = jnp.sum(inbox[...], axis=0)
    ones_at = (FIELDS + 1) * levels
    means = total / jnp.broadcast_to(total[:, ones_at : ones_at + 1], total.shape)
    zonal[...] = means[:, : FIELDS * levels]
    lane = lax.broadcasted_iota(jnp.int32, means.shape, 1)
    k = 1
    while k < levels:
        means = means + jnp.where(lane >= FIELDS * levels + k, pltpu.roll(means, k, 1), 0.0)
        k *= 2
    lat_row = me * BAND_ROWS + lax.broadcasted_iota(jnp.int32, means.shape, 0)
    total_rows = BAND_ROWS * devices
    phi = ((lat_row.astype(f32) + 0.5) / total_rows - 0.5) * (jnp.pi / 2)
    means = jnp.cos(phi) * means
    stream[...] = means[:, FIELDS * levels : ones_at]

    for g in range(groups):
        for side in range(2):
            halo_copy(side, g).wait_send()
    others.wait_send()
    for store in stores:
        store.wait()


def on_device(n_face, n_tile, state, wave, turns, mass, source, row, weight, count):
    fields, levels, cols, width = state.shape
    halo = SUBSTEPS
    groups = levels // GROUP
    devices = n_face * n_tile
    slots = source.shape[2]
    merged = (fields, levels * cols, width)
    smem = pl.BlockSpec(memory_space=pltpu.SMEM)
    vmem = pl.BlockSpec(memory_space=pltpu.VMEM)
    hbm = pl.BlockSpec(memory_space=pl.ANY)
    field = pltpu.VMEM((groups, cols + 2 * halo, fields, GROUP, width), f32)
    dma = pltpu.SemaphoreType.DMA

    def body(*refs):
        kernel(n_face, n_tile, cols, halo, *refs)

    new_state, zonal, stream = pl.pallas_call(
        body,
        out_shape=(
            jax.ShapeDtypeStruct(merged, f32),
            jax.ShapeDtypeStruct((BAND_ROWS, fields * levels), f32),
            jax.ShapeDtypeStruct((BAND_ROWS, levels), f32),
        ),
        in_specs=[smem, smem, smem, smem, hbm, hbm, hbm, hbm],
        out_specs=(hbm, vmem, vmem),
        scratch_shapes=[
            field,
            field,
            field,
            pltpu.VMEM((fields, width // LANES, levels * cols, LANES), f32),
            pltpu.VMEM((cols * width, LANES), f32),
            pltpu.VMEM((2, GATHERED, slots, LANES), f32),
            pltpu.VMEM((groups, GROUP, LANES), f32),
            pltpu.VMEM((groups, GROUP, LANES), f32),
            pltpu.VMEM((devices, slots), jnp.int32),
            pltpu.VMEM((devices, slots), f32),
            pltpu.SMEM((GATHERED, slots), jnp.int32),
            pltpu.SMEM((GATHERED, slots), jnp.int32),
            pltpu.VMEM((devices, BAND_ROWS, LANES), f32),
            pltpu.VMEM((devices, BAND_ROWS, LANES), f32),
            dma((width // LANES,)),
            dma,
            dma,
            dma((width // LANES,)),
            dma((2,)),
            dma((2, groups)),
            dma((2, groups)),
            dma,
            dma,
        ],
        compiler_params=pltpu.CompilerParams(
            collective_id=1, has_side_effects=True, vmem_limit_bytes=56 * 2**20
        ),
    )(
        wave,
        turns,
        mass,
        count[0],
        state.reshape(merged),
        source[0],
        row[0],
        weight[0],
    )
    return new_state.reshape(state.shape), zonal, stream


def solution(mesh):
    n_face, n_tile = mesh.shape["face"], mesh.shape["tile"]
    both = ("face", "tile")
    zonal_dim = P(None, None, both, None)
    links = P(both, None, None)

    def program(*args):
        return on_device(n_face, n_tile, *args)

    return jax.shard_map(
        program,
        mesh=mesh,
        in_specs=(zonal_dim, P(), P(), P(), links, links, links, P(both, None)),
        out_specs=(zonal_dim, P(both, None), P(both, None)),
        check_vma=False,
    )
```

profile of v0, /device:TPU:2, one launch (start us, length us, event | category | flops | bytes accessed | tf_op | source)
XLA Modules:
  0.0 60.0 jit_solution(6556459268868452778)
XLA Ops:
  0.6 53.3 %shard_map.103 = (f32[4,384,768]{2,1,0:T(8,128)}, f32[4,64]{1,0:T(4,128)}, f32[4,16]{1,0:T(4,128)}) custom-call(f32[16]{0:T(128)} %refs_0_.1, s32[4]{0:T(128)} %refs_1_.1, f32[16]{0:T(128)} %refs_2_.1, s32[128]{0:T(128)} %bitcast.11, f32[4,384,768]{2,1,0:T(8,128)} %bitcast.6, s32[128,128]{1,0:T(8,128)} %bitcast.8, s32[128,128]{1,0:T(8,128)} %bitcast.9, ...), custom_call_target="tpu_custom_call" | custom-call | tf_op jit(solution)/shard_map/pallas_call | solution.py:384
  53.9 0.0 copy-start.1
  53.9 0.0 copy-start
  53.9 4.9 %copy.14 = f32[4,16,24,768]{3,2,1,0:T(8,128)} copy(f32[4,16,24,768]{3,2,1,0:T(8,128)} %bitcast.7) | data formatting | bytes 9437184
  58.8 0.0 copy-done.1
  58.8 0.6 copy.15
  59.4 0.0 copy-done
  59.4 0.6 copy.16
Async XLA Ops:
  53.9 4.9 %copy-start.1 = (f32[4,64]{1,0:T(4,128)S(1)}, f32[4,64]{1,0:T(4,128)}, u32[]{:S(2)}) copy-start(f32[4,64]{1,0:T(4,128)} %get-tuple-element.13) | copy-start | bytes 3076
  53.9 5.5 %copy-start = (f32[4,16]{1,0:T(4,128)S(1)}, f32[4,16]{1,0:T(4,128)}, u32[]{:S(2)}) copy-start(f32[4,16]{1,0:T(4,128)} %get-tuple-element.14) | copy-start | bytes 772
where the time goes:
time: 61.1 us; the launch traced here: 60 us
  Pallas kernels  53.3 us (87%)
  local copies, waits for them, and re-layouts  6.05 us (10%)
  between operations  0.66 us (1%)
    pallas_call x1, Pallas kernels, on_device(): pl.pallas_call(body, out_shape=(jax.ShapeDtypeStruct(merged, f32), jax.Sh...  53.3 us
    unnamed x7, local copies, waits for them, and re-layouts  6.05 us

commit v1 on v0

--- a/solution.py
+++ b/solution.py
@@ -11,27 +11,11 @@
 GROUP = 8
 LANES = 128
 GATHERED = 8
+HANDED = 16
 SCALE = 10.0**-SUBSTEPS
 
 f32 = jnp.float32
 bf16 = jnp.bfloat16
-
-
-def north_of(q):
-    width = q.shape[1]
-    rolled = pltpu.roll(q, width - 1, 1)
-    tail = rolled[:, width - LANES :]
-    lane = lax.broadcasted_iota(jnp.int32, tail.shape, 1)
-    tail = jnp.where(lane == LANES - 1, 0.0, tail)
-    return jnp.concatenate([rolled[:, : width - LANES], tail], axis=1)
-
-
-def south_of(q):
-    rolled = pltpu.roll(q, 1, 1)
-    head = rolled[:, :LANES]
-    lane = lax.broadcasted_iota(jnp.int32, head.shape, 1)
-    head = jnp.where(lane == 0, 0.0, head)
-    return jnp.concatenate([head, rolled[:, LANES:]], axis=1)
 
 
 def turned(wind, turn):
@@ -40,27 +24,59 @@
     return cosine * east - sine * north, sine * east + cosine * north
 
 
-def column(source, target, group, at, courant, turn_west=None, turn_east=None):
-    mid = [source[group, at, c] for c in range(FIELDS)]
-    west = [source[group, at - 1, c] for c in range(FIELDS)]
-    east = [source[group, at + 1, c] for c in range(FIELDS)]
-    if turn_west is not None:
-        west[0], west[1] = turned(west[:2], turn_west)
-    if turn_east is not None:
-        east[0], east[1] = turned(east[:2], turn_east)
-    north = [north_of(q) for q in mid]
-    south = [south_of(q) for q in mid]
-    base = [
-        6.0 * mid[c] + ((west[c] + east[c]) + (north[c] + south[c]))
-        for c in range(FIELDS)
-    ]
-    spread = courant * ((east[0] - west[0]) + (north[1] - south[1]))
-    push_x = courant * ((east[3] - west[3]) + (east[2] - west[2]))
-    push_y = courant * ((north[3] - south[3]) + (north[2] - south[2]))
-    target[group, at, 0] = base[0] - push_x
-    target[group, at, 1] = base[1] - push_y
-    target[group, at, 2] = base[2] - 0.25 * spread
-    target[group, at, 3] = base[3] - spread
+def strip(source, target, group, at, count, courant, turns=None):
+    turns = turns or {}
+    blocks = source.shape[4] // LANES
+    lane = lax.broadcasted_iota(jnp.int32, (GROUP, LANES), 1)
+    first_lane, last_lane = lane == 0, lane == LANES - 1
+    inside = range(count)
+
+    def mids(j):
+        return {
+            (k, c): source[group, at + k, c, :, pl.ds(j * LANES, LANES)]
+            for k in inside
+            for c in range(FIELDS)
+        }
+
+    def rolls(mid, amount):
+        return {key: pltpu.roll(q, amount, 1) for key, q in mid.items()}
+
+    mid = mids(0)
+    up, down = rolls(mid, LANES - 1), rolls(mid, 1)
+    zeros = {key: jnp.zeros((GROUP, LANES), f32) for key in mid}
+    down_before = zeros
+    for j in range(blocks):
+        if j + 1 < blocks:
+            mid_next = mids(j + 1)
+            up_next, down_next = rolls(mid_next, LANES - 1), rolls(mid_next, 1)
+        else:
+            mid_next, up_next, down_next = None, zeros, None
+        here = dict(mid)
+        for k in (-1, count):
+            for c in range(FIELDS):
+                here[k, c] = source[group, at + k, c, :, pl.ds(j * LANES, LANES)]
+        for k in inside:
+            west = [here[k - 1, c] for c in range(FIELDS)]
+            east = [here[k + 1, c] for c in range(FIELDS)]
+            if k - 1 in turns:
+                west[:2] = turned(west[:2], turns[k - 1])
+            if k in turns:
+                cosine, sine = turns[k]
+                east[:2] = turned(east[:2], (cosine, -sine))
+            north = [jnp.where(last_lane, up_next[k, c], up[k, c]) for c in range(FIELDS)]
+            south = [jnp.where(first_lane, down_before[k, c], down[k, c]) for c in range(FIELDS)]
+            base = [
+                6.0 * mid[k, c] + ((west[c] + east[c]) + (north[c] + south[c]))
+                for c in range(FIELDS)
+            ]
+            spread = courant * ((east[0] - west[0]) + (north[1] - south[1]))
+            push_x = courant * ((east[3] - west[3]) + (east[2] - west[2]))
+            push_y = courant * ((north[3] - south[3]) + (north[2] - south[2]))
+            out = [base[0] - push_x, base[1] - push_y, base[2] - 0.25 * spread, base[3] - spread]
+            for c in range(FIELDS):
+                target[group, at + k, c, :, pl.ds(j * LANES, LANES)] = out[c]
+        mid, down_before = mid_next, down
+        up, down = up_next, down_next
 
 
 def quarter(code):
@@ -84,11 +100,11 @@
 
 def kernel(
     n_face, n_tile, cols, halo,
-    wave, turns, mass, counts, state, source, row, weight,
-    new_state, zonal, stream,
+    wave_in, turns_in, mass_in, counts_in, state, source, row, weight,
+    fields_out, means_out,
     first, odd, even, slab, cells, picked, courants, masses, rows, weights,
-    spots0, spots1, sums, inbox,
-    load_sem, row_sem, weight_sem, store_sem, spot_sem, send_sem, recv_sem,
+    spots0, spots1, sums, inbox, wave, turns, mass, counts,
+    load_sem, row_sem, weight_sem, scalar_sem, store_sem, spot_sem, send_sem, recv_sem,
     out_sem, in_sem,
 ):
     face, tile = lax.axis_index("face"), lax.axis_index("tile")
@@ -106,11 +122,11 @@
 
     right, left = place(me + 1), place(me + devices - 1)
 
-    def strip(ref, j):
+    def lanes_of(ref, j):
         return ref.at[:, :, pl.ds(j * LANES, LANES)]
 
     loads = [
-        pltpu.make_async_copy(strip(state, j), slab.at[:, j], load_sem.at[j])
+        pltpu.make_async_copy(lanes_of(state, j), slab.at[:, j], load_sem.at[j])
         for j in range(repeat)
     ]
     for load in loads:
@@ -120,6 +136,14 @@
     weight_load = pltpu.make_async_copy(weight, weights, weight_sem)
     weight_load.start()
 
+    scalars = [(wave_in, wave), (turns_in, turns), (mass_in, mass), (counts_in, counts)]
+    scalar_loads = [
+        pltpu.make_async_copy(there, here, scalar_sem.at[k])
+        for k, (there, here) in enumerate(scalars)
+    ]
+    for scalar_load in scalar_loads:
+        scalar_load.start()
+
     barrier = pltpu.get_barrier_semaphore()
 
     def greet(i, carry):
@@ -128,6 +152,8 @@
 
     lax.fori_loop(1, devices, greet, 0)
 
+    for scalar_load in scalar_loads:
+        scalar_load.wait()
     for g in range(groups):
         courants[g] = 5.0 * per_level(wave, g)
         masses[g] = per_level(mass, g)
@@ -154,23 +180,28 @@
 
     pl.semaphore_wait(barrier, devices - 1)
 
-    def halo_copy(side, g):
+    messages = [(g, 1, halo) for g in range(groups - 1)]
+    messages += [(groups - 1, k, 1) for k in range(1, halo + 1)]
+
+    def halo_copy(side, m):
+        g, k, count = messages[m]
+        far = k + count - 1
         if side == 0:
-            here, there, to = cols, 0, right
+            here, there, to = cols + halo - far, halo - far, right
         else:
-            here, there, to = halo, cols + halo, left
+            here, there, to = halo + k - 1, cols + halo + k - 1, left
         return pltpu.make_async_remote_copy(
-            src_ref=first.at[g, pl.ds(here, halo)],
-            dst_ref=first.at[g, pl.ds(there, halo)],
-            send_sem=send_sem.at[side, g],
-            recv_sem=recv_sem.at[side, g],
+            src_ref=first.at[g, pl.ds(here, count)],
+            dst_ref=first.at[g, pl.ds(there, count)],
+            send_sem=send_sem.at[side, m],
+            recv_sem=recv_sem.at[side, m],
             device_id=to,
             device_id_type=mesh_id,
         )
 
-    for g in range(groups):
+    for m in range(len(messages)):
         for side in range(2):
-            halo_copy(side, g).start()
+            halo_copy(side, m).start()
 
     def lift_inner(i, carry):
         n = cols - 2 * halo
@@ -182,16 +213,13 @@
     steps = [(first, odd), (odd, even), (even, odd), (odd, even)]
 
     for s, (old, new) in enumerate(steps, 1):
-        n = cols - 2 * s
-
-        def inner(i, carry, old=old, new=new, s=s, n=n):
-            g, x = lax.div(i, n), lax.rem(i, n)
-            column(old, new, g, x + s + halo, wide(courants[g]))
+
+        def inner(g, carry, old=old, new=new, s=s):
+            for x in range(s, cols - s, 2):
+                strip(old, new, g, x + halo, 2, courants[g])
             return carry
 
-        lax.fori_loop(0, groups * n, inner, 0, unroll=2)
-
-    lane = lax.broadcasted_iota(jnp.int32, (GROUP, width), 1)
+        lax.fori_loop(0, groups, inner, 0)
 
     def finish(x):
         values = {}
@@ -219,37 +247,25 @@
     west_cos, west_sin = quarter(jnp.where(tile == 0, turns[face], 0))
     east_cos, east_sin = quarter(jnp.where(tile == n_tile - 1, turns[lax.rem(face + 1, n_face)], 0))
 
-    def edges(g, carry):
-        courant = wide(courants[g])
-        halo_copy(0, g).wait_recv()
+    west_turn, east_turn = (west_cos, west_sin), (east_cos, east_sin)
+    for m, (g, k, count) in enumerate(messages):
+        halo_copy(0, m).wait_recv()
+        halo_copy(1, m).wait_recv()
+        if count == halo:
+            for s, (old, new) in enumerate(steps, 1):
+                strip(old, new, g, s, halo, courants[g], {halo - 1 - s: west_turn})
+                strip(old, new, g, cols - s + halo, halo, courants[g], {s - 1: east_turn})
+            continue
         for s, (old, new) in enumerate(steps, 1):
-            for x in range(s - halo, s):
-                column(
-                    old, new, g, x + halo, courant,
-                    turn_west=(west_cos, west_sin) if x == 0 else None,
-                    turn_east=(west_cos, -west_sin) if x == -1 else None,
-                )
-        halo_copy(1, g).wait_recv()
-        for s, (old, new) in enumerate(steps, 1):
-            for x in range(cols - s, cols + halo - s):
-                column(
-                    old, new, g, x + halo, courant,
-                    turn_west=(east_cos, east_sin) if x == cols else None,
-                    turn_east=(east_cos, -east_sin) if x == cols - 1 else None,
-                )
-        return carry
-
-    for g in range(groups):
-        edges(g, 0)
-
-    def finish_edge(i, carry):
-        finish(i + (cols - 2 * halo) * lax.div(i, halo))
-        return carry
-
-    lax.fori_loop(0, 2 * halo, finish_edge, 0)
+            x = s - k
+            strip(old, new, g, x + halo, 1, courants[g], {-1 - x: west_turn})
+            x = cols - 1 + k - s
+            strip(old, new, g, x + halo, 1, courants[g], {cols - 1 - x: east_turn})
+        finish(halo - k)
+        finish(cols - 1 - halo + k)
 
     stores = [
-        pltpu.make_async_copy(slab.at[:, j], strip(new_state, j), store_sem.at[j])
+        pltpu.make_async_copy(slab.at[:, j], lanes_of(fields_out, j), store_sem.at[j])
         for j in range(repeat)
     ]
     for store in stores:
@@ -262,7 +278,7 @@
     slots = rows.shape[1]
 
     def first_band(turn):
-        return pl.multiple_of(lax.rem(lax.div(me, GATHERED) + turn, rounds) * GATHERED, GATHERED)
+        return pl.multiple_of(lax.rem(lax.div(me, GATHERED) + 1 + turn, rounds) * GATHERED, GATHERED)
 
     def spot_copy(turn, slot):
         return pltpu.make_async_copy(
@@ -297,6 +313,9 @@
                 + product[:BAND_ROWS, LANES:]
                 + product[BAND_ROWS:, :LANES]
             )
+
+    def send(turn):
+        start = first_band(turn)
         for k in range(GATHERED):
             band = start + k
 
@@ -317,21 +336,31 @@
 
     spot_copy(0, 0).start()
     spot_copy(1, 1).start()
+    spot_copy(0, 0).wait()
+    pick(0)
+    spot_copy(2, 0).start()
 
     def two_rounds(i, carry):
-        for slot in range(2):
-            turn = 2 * i + slot
+        for slot in (1, 0):
+            turn = 2 * i + 2 - slot
             spot_copy(turn, slot).wait()
             pick(slot)
+            add_up(turn - 1, 1 - slot)
 
             @pl.when(turn + 2 < rounds)
             def _():
                 spot_copy(turn + 2, slot).start()
 
-            add_up(turn, slot)
+            send(turn - 1)
         return carry
 
-    lax.fori_loop(0, rounds // 2, two_rounds, 0)
+    lax.fori_loop(0, rounds // 2 - 1, two_rounds, 0)
+    spot_copy(rounds - 1, 1).wait()
+    pick(1)
+    add_up(rounds - 2, 0)
+    send(rounds - 2)
+    add_up(rounds - 1, 1)
+    send(rounds - 1)
 
     others = pltpu.make_async_remote_copy(
         src_ref=sums.at[pl.ds(0, devices - 1)],
@@ -345,7 +374,7 @@
     total = jnp.sum(inbox[...], axis=0)
     ones_at = (FIELDS + 1) * levels
     means = total / jnp.broadcast_to(total[:, ones_at : ones_at + 1], total.shape)
-    zonal[...] = means[:, : FIELDS * levels]
+    zonal = means
     lane = lax.broadcasted_iota(jnp.int32, means.shape, 1)
     k = 1
     while k < levels:
@@ -354,13 +383,40 @@
     lat_row = me * BAND_ROWS + lax.broadcasted_iota(jnp.int32, means.shape, 0)
     total_rows = BAND_ROWS * devices
     phi = ((lat_row.astype(f32) + 0.5) / total_rows - 0.5) * (jnp.pi / 2)
-    means = jnp.cos(phi) * means
-    stream[...] = means[:, FIELDS * levels : ones_at]
-
-    for g in range(groups):
+    stream = jnp.cos(phi) * means
+    means_out[...] = jnp.where(lane < FIELDS * levels, zonal, stream)
+
+    for m in range(len(messages)):
         for side in range(2):
-            halo_copy(side, g).wait_send()
+            halo_copy(side, m).wait_send()
     others.wait_send()
+    for store in stores:
+        store.wait()
+
+
+def hand_over(fields_in, means, new_state, zonal, stream, held, in_sem, out_sem):
+    parts, length = held.shape[0], held.shape[2]
+    per_field = parts // FIELDS
+
+    def piece(ref, k):
+        return ref.at[k // per_field, pl.ds(k % per_field * length, length)]
+
+    loads = [
+        pltpu.make_async_copy(piece(fields_in, k), held.at[k, 0], in_sem.at[k])
+        for k in range(parts)
+    ]
+    stores = [
+        pltpu.make_async_copy(held.at[k, 0], piece(new_state, k), out_sem.at[k])
+        for k in range(parts)
+    ]
+    for load in loads:
+        load.start()
+    count = zonal.shape[1]
+    zonal[...] = means[:, :count]
+    stream[...] = means[:, count : count + stream.shape[1]]
+    for load, store in zip(loads, stores):
+        load.wait()
+        store.start()
     for store in stores:
         store.wait()
 
@@ -372,24 +428,22 @@
     devices = n_face * n_tile
     slots = source.shape[2]
     merged = (fields, levels * cols, width)
-    smem = pl.BlockSpec(memory_space=pltpu.SMEM)
     vmem = pl.BlockSpec(memory_space=pltpu.VMEM)
-    hbm = pl.BlockSpec(memory_space=pl.ANY)
+    hbm = pl.BlockSpec(memory_space=pltpu.HBM)
     field = pltpu.VMEM((groups, cols + 2 * halo, fields, GROUP, width), f32)
     dma = pltpu.SemaphoreType.DMA
 
     def body(*refs):
         kernel(n_face, n_tile, cols, halo, *refs)
 
-    new_state, zonal, stream = pl.pallas_call(
+    new_fields, means = pl.pallas_call(
         body,
         out_shape=(
             jax.ShapeDtypeStruct(merged, f32),
-            jax.ShapeDtypeStruct((BAND_ROWS, fields * levels), f32),
-            jax.ShapeDtypeStruct((BAND_ROWS, levels), f32),
+            jax.ShapeDtypeStruct((BAND_ROWS, LANES), f32),
         ),
-        in_specs=[smem, smem, smem, smem, hbm, hbm, hbm, hbm],
-        out_specs=(hbm, vmem, vmem),
+        in_specs=[hbm] * 8,
+        out_specs=(hbm, vmem),
         scratch_shapes=[
             field,
             field,
@@ -405,18 +459,23 @@
             pltpu.SMEM((GATHERED, slots), jnp.int32),
             pltpu.VMEM((devices, BAND_ROWS, LANES), f32),
             pltpu.VMEM((devices, BAND_ROWS, LANES), f32),
+            pltpu.SMEM((levels,), f32),
+            pltpu.SMEM((n_face,), jnp.int32),
+            pltpu.SMEM((levels,), f32),
+            pltpu.SMEM((devices,), jnp.int32),
             dma((width // LANES,)),
             dma,
             dma,
+            dma((4,)),
             dma((width // LANES,)),
             dma((2,)),
-            dma((2, groups)),
-            dma((2, groups)),
+            dma((2, groups - 1 + halo)),
+            dma((2, groups - 1 + halo)),
             dma,
             dma,
         ],
         compiler_params=pltpu.CompilerParams(
-            collective_id=1, has_side_effects=True, vmem_limit_bytes=56 * 2**20
+            collective_id=1, has_side_effects=True, vmem_limit_bytes=57 * 2**20
         ),
     )(
         wave,
@@ -428,6 +487,22 @@
         row[0],
         weight[0],
     )
+    new_state, zonal, stream = pl.pallas_call(
+        hand_over,
+        out_shape=(
+            jax.ShapeDtypeStruct(merged, f32),
+            jax.ShapeDtypeStruct((BAND_ROWS, fields * levels), f32),
+            jax.ShapeDtypeStruct((BAND_ROWS, levels), f32),
+        ),
+        in_specs=[hbm, vmem],
+        out_specs=(hbm, vmem, vmem),
+        scratch_shapes=[
+            pltpu.VMEM((HANDED, 1, fields * levels * cols // HANDED, width), f32),
+            dma((HANDED,)),
+            dma((HANDED,)),
+        ],
+        compiler_params=pltpu.CompilerParams(vmem_limit_bytes=57 * 2**20),
+    )(new_fields, means)
     return new_state.reshape(state.shape), zonal, stream
 
 

time: 61.1 us -> 56.5 us (0.925)
  local copies, waits for them, and re-layouts: 6.05 us -> 0 us
  Pallas kernels: 53.3 us -> 54.9 us
    unnamed x7 -> x0, local copies, waits for them, and re-layouts: 6.05 us -> none
    pallas_call x0 -> x1, Pallas kernels: none -> 5.63 us  [on_device(): pl.pallas_call(hand_over, out_shape=(jax.ShapeDtypeStruct(merged, f32), j...]
    pallas_call x1, Pallas kernels: 53.3 us -> 49.3 us  [on_device(): pl.pallas_call(body, out_shape=(jax.ShapeDtypeStruct(merged, f32), jax.Sh...]
where the time goes in v1:
time: 56.5 us; the launch traced here: 55.5 us
  Pallas kernels  54.9 us (97%)
  between operations  0.64 us (1%)
    pallas_call x1, Pallas kernels, on_device(): pl.pallas_call(body, out_shape=(jax.ShapeDtypeStruct(merged, f32), jax.Sh...  49.3 us
    pallas_call x1, Pallas kernels, on_device(): pl.pallas_call(hand_over, out_shape=(jax.ShapeDtypeStruct(merged, f32), j...  5.63 us

profile of v1, /device:TPU:2, one launch (start us, length us, event | category | flops | bytes accessed | tf_op | source)
XLA Modules:
  0.0 55.5 jit_solution(12820090869003854126)
XLA Ops:
  0.6 49.3 %shard_map.103 = (f32[4,384,768]{2,1,0:T(8,128)}, f32[4,128]{1,0:T(4,128)}) custom-call(f32[16]{0:T(128)} %refs_0_.1, s32[4]{0:T(128)} %refs_1_.1, f32[16]{0:T(128)} %refs_2_.1, s32[128]{0:T(128)} %bitcast.10, f32[4,384,768]{2,1,0:T(8,128)} %bitcast.6, s32[128,128]{1,0:T(8,128)} %bitcast.7, s32[128,128]{1,0:T(8,128)} %bitcast.8, f32[128,128]{1,0:T(8,128)} %bitcast.9), custom_call_target="tpu_custom_call" | custom-call | tf_op jit(solution)/shard_map/pallas_call | solution.py:439
  49.9 5.6 %shard_map.104 = (f32[4,384,768]{2,1,0:T(8,128)}, f32[4,64]{1,0:T(4,128)}, f32[4,16]{1,0:T(4,128)}) custom-call(f32[4,384,768]{2,1,0:T(8,128)} %get-tuple-element.8.fields_in, f32[4,128]{1,0:T(4,128)} %get-tuple-element.9.means), custom_call_target="tpu_custom_call" | custom-call | tf_op jit(solution)/shard_map/pallas_call | solution.py:490

commit v2 on v1

--- a/solution.py
+++ b/solution.py
@@ -105,7 +105,7 @@
     first, odd, even, slab, cells, picked, courants, masses, rows, weights,
     spots0, spots1, sums, inbox, wave, turns, mass, counts,
     load_sem, row_sem, weight_sem, scalar_sem, store_sem, spot_sem, send_sem, recv_sem,
-    out_sem, in_sem,
+    out_sem, in_sem, meet,
 ):
     face, tile = lax.axis_index("face"), lax.axis_index("tile")
     devices = n_face * n_tile
@@ -146,11 +146,20 @@
 
     barrier = pltpu.get_barrier_semaphore()
 
-    def greet(i, carry):
-        pl.semaphore_signal(barrier, inc=1, device_id=place(me + i), device_id_type=mesh_id)
-        return carry
-
-    lax.fori_loop(1, devices, greet, 0)
+    def partner(b):
+        bit = lax.rem(lax.div(me, 1 << b), 2)
+        return place(me + (1 - 2 * bit) * (1 << b))
+
+    partners = devices.bit_length() - 1
+    greeted = [right, left] + [partner(b) for b in range(partners)]
+    for device in greeted:
+        pl.semaphore_signal(barrier, inc=1, device_id=device, device_id_type=mesh_id)
+
+    def tell(b):
+        pl.semaphore_signal(meet.at[b], inc=1, device_id=partner(b), device_id_type=mesh_id)
+
+    def hear(b):
+        pl.semaphore_wait(meet.at[b], 1)
 
     for scalar_load in scalar_loads:
         scalar_load.wait()
@@ -178,7 +187,7 @@
 
     lax.fori_loop(0, groups * 2 * halo, lift_edge, 0)
 
-    pl.semaphore_wait(barrier, devices - 1)
+    pl.semaphore_wait(barrier, len(greeted))
 
     messages = [(g, 1, halo) for g in range(groups - 1)]
     messages += [(groups - 1, k, 1) for k in range(1, halo + 1)]
@@ -202,6 +211,20 @@
     for m in range(len(messages)):
         for side in range(2):
             halo_copy(side, m).start()
+    tell(0)
+    met = 0
+
+    spots = (spots0, spots1)
+    rounds = devices // GATHERED
+    slots = rows.shape[1]
+
+    def first_band(turn):
+        return pl.multiple_of(lax.rem(lax.div(me, GATHERED) + 1 + turn, rounds) * GATHERED, GATHERED)
+
+    def spot_copy(turn, slot):
+        return pltpu.make_async_copy(
+            source.at[pl.ds(first_band(turn), GATHERED)], spots[slot], spot_sem.at[slot]
+        )
 
     def lift_inner(i, carry):
         n = cols - 2 * halo
@@ -209,6 +232,8 @@
         return carry
 
     lax.fori_loop(0, groups * (cols - 2 * halo), lift_inner, 0)
+    spot_copy(0, 0).start()
+    spot_copy(1, 1).start()
 
     steps = [(first, odd), (odd, even), (even, odd), (odd, even)]
 
@@ -220,6 +245,10 @@
             return carry
 
         lax.fori_loop(0, groups, inner, 0)
+        if met + 1 < partners:
+            hear(met)
+            met += 1
+            tell(met)
 
     def finish(x):
         values = {}
@@ -244,6 +273,11 @@
 
     lax.fori_loop(0, cols - 2 * halo, finish_inner, 0)
 
+    while met + 1 < partners:
+        hear(met)
+        met += 1
+        tell(met)
+
     west_cos, west_sin = quarter(jnp.where(tile == 0, turns[face], 0))
     east_cos, east_sin = quarter(jnp.where(tile == n_tile - 1, turns[lax.rem(face + 1, n_face)], 0))
 
@@ -273,18 +307,7 @@
 
     row_load.wait()
     weight_load.wait()
-    spots = (spots0, spots1)
-    rounds = devices // GATHERED
-    slots = rows.shape[1]
-
-    def first_band(turn):
-        return pl.multiple_of(lax.rem(lax.div(me, GATHERED) + 1 + turn, rounds) * GATHERED, GATHERED)
-
-    def spot_copy(turn, slot):
-        return pltpu.make_async_copy(
-            source.at[pl.ds(first_band(turn), GATHERED)], spots[slot], spot_sem.at[slot]
-        )
-
+    hear(met)
     def pick(slot):
         for k in range(GATHERED):
             for j in range(slots):
@@ -334,8 +357,6 @@
             def _():
                 inbox[me] = sums[band]
 
-    spot_copy(0, 0).start()
-    spot_copy(1, 1).start()
     spot_copy(0, 0).wait()
     pick(0)
     spot_copy(2, 0).start()
@@ -370,6 +391,10 @@
         device_id=right,
         device_id_type=mesh_id,
     )
+    lat_row = me * BAND_ROWS + lax.broadcasted_iota(jnp.int32, (BAND_ROWS, LANES), 0)
+    total_rows = BAND_ROWS * devices
+    phi = ((lat_row.astype(f32) + 0.5) / total_rows - 0.5) * (jnp.pi / 2)
+    cosine = jnp.cos(phi)
     others.wait_recv()
     total = jnp.sum(inbox[...], axis=0)
     ones_at = (FIELDS + 1) * levels
@@ -380,10 +405,7 @@
     while k < levels:
         means = means + jnp.where(lane >= FIELDS * levels + k, pltpu.roll(means, k, 1), 0.0)
         k *= 2
-    lat_row = me * BAND_ROWS + lax.broadcasted_iota(jnp.int32, means.shape, 0)
-    total_rows = BAND_ROWS * devices
-    phi = ((lat_row.astype(f32) + 0.5) / total_rows - 0.5) * (jnp.pi / 2)
-    stream = jnp.cos(phi) * means
+    stream = cosine * means
     means_out[...] = jnp.where(lane < FIELDS * levels, zonal, stream)
 
     for m in range(len(messages)):
@@ -473,6 +495,7 @@
             dma((2, groups - 1 + halo)),
             dma,
             dma,
+            pltpu.SemaphoreType.REGULAR((devices.bit_length() - 1,)),
         ],
         compiler_params=pltpu.CompilerParams(
             collective_id=1, has_side_effects=True, vmem_limit_bytes=57 * 2**20

time: 56.5 us -> 51.5 us (0.912); the launches traced: 55.5 us -> 51.3 us
  Pallas kernels: 54.9 us -> 50.7 us
    pallas_call x1, Pallas kernels: 49.3 us -> 45 us  [on_device(): pl.pallas_call(body, out_shape=(jax.ShapeDtypeStruct(merged, f32), jax.Sh...]
where the time goes in v2:
time: 51.5 us; the launch traced here: 51.3 us
  Pallas kernels  50.7 us (98%)
  between operations  0.64 us (1%)
    pallas_call x1, Pallas kernels, on_device(): pl.pallas_call(body, out_shape=(jax.ShapeDtypeStruct(merged, f32), jax.Sh...  45 us
    pallas_call x1, Pallas kernels, on_device(): pl.pallas_call(hand_over, out_shape=(jax.ShapeDtypeStruct(merged, f32), j...  5.63 us

profile of v2, /device:TPU:2, one launch (start us, length us, event | category | flops | bytes accessed | tf_op | source)
XLA Modules:
  0.0 51.3 jit_solution(3973017817359513221)
XLA Ops:
  0.6 45.0 %shard_map.103 = (f32[4,384,768]{2,1,0:T(8,128)}, f32[4,128]{1,0:T(4,128)}) custom-call(f32[16]{0:T(128)} %refs_0_.1, s32[4]{0:T(128)} %refs_1_.1, f32[16]{0:T(128)} %refs_2_.1, s32[128]{0:T(128)} %bitcast.10, f32[4,384,768]{2,1,0:T(8,128)} %bitcast.6, s32[128,128]{1,0:T(8,128)} %bitcast.7, s32[128,128]{1,0:T(8,128)} %bitcast.8, f32[128,128]{1,0:T(8,128)} %bitcast.9), custom_call_target="tpu_custom_call" | custom-call | tf_op jit(solution)/shard_map/pallas_call | solution.py:461
  45.7 5.6 %shard_map.104 = (f32[4,384,768]{2,1,0:T(8,128)}, f32[4,64]{1,0:T(4,128)}, f32[4,16]{1,0:T(4,128)}) custom-call(f32[4,384,768]{2,1,0:T(8,128)} %get-tuple-element.8.fields_in, f32[4,128]{1,0:T(4,128)} %get-tuple-element.9.means), custom_call_target="tpu_custom_call" | custom-call | tf_op jit(solution)/shard_map/pallas_call | solution.py:513

commit v3 on v2

--- a/solution.py
+++ b/solution.py
@@ -337,25 +337,24 @@
                 + product[BAND_ROWS:, :LANES]
             )
 
+    def send_band(band):
+        pltpu.make_async_remote_copy(
+            src_ref=sums.at[band],
+            dst_ref=inbox.at[me],
+            send_sem=out_sem,
+            recv_sem=in_sem,
+            device_id=place(band),
+            device_id_type=mesh_id,
+        ).start()
+
     def send(turn):
-        start = first_band(turn)
         for k in range(GATHERED):
-            band = start + k
-
-            @pl.when(band != me)
-            def _():
-                pltpu.make_async_remote_copy(
-                    src_ref=sums.at[band],
-                    dst_ref=inbox.at[me],
-                    send_sem=out_sem,
-                    recv_sem=in_sem,
-                    device_id=place(band),
-                    device_id_type=mesh_id,
-                ).start()
-
-            @pl.when(band == me)
-            def _():
-                inbox[me] = sums[band]
+            send_band(first_band(turn) + k)
+
+    def send_last():
+        for k in range(1, GATHERED):
+            send_band(first_band(rounds - 1) + lax.rem(me + k, GATHERED))
+        inbox[me] = sums[me]
 
     spot_copy(0, 0).wait()
     pick(0)
@@ -381,7 +380,7 @@
     add_up(rounds - 2, 0)
     send(rounds - 2)
     add_up(rounds - 1, 1)
-    send(rounds - 1)
+    send_last()
 
     others = pltpu.make_async_remote_copy(
         src_ref=sums.at[pl.ds(0, devices - 1)],
@@ -416,7 +415,10 @@
         store.wait()
 
 
-def hand_over(fields_in, means, new_state, zonal, stream, held, in_sem, out_sem):
+def hand_over(
+    fields_in, means_in, new_state, zonal_out, stream_out,
+    held, means, zonal, stream, in_sem, out_sem, small_sem,
+):
     parts, length = held.shape[0], held.shape[2]
     per_field = parts // FIELDS
 
@@ -431,15 +433,22 @@
         pltpu.make_async_copy(held.at[k, 0], piece(new_state, k), out_sem.at[k])
         for k in range(parts)
     ]
+    load_means = pltpu.make_async_copy(means_in, means, small_sem.at[0])
+    store_zonal = pltpu.make_async_copy(zonal, zonal_out, small_sem.at[1])
+    store_stream = pltpu.make_async_copy(stream, stream_out, small_sem.at[2])
+    load_means.start()
     for load in loads:
         load.start()
+    load_means.wait()
     count = zonal.shape[1]
     zonal[...] = means[:, :count]
     stream[...] = means[:, count : count + stream.shape[1]]
+    store_zonal.start()
+    store_stream.start()
     for load, store in zip(loads, stores):
         load.wait()
         store.start()
-    for store in stores:
+    for store in [store_zonal, store_stream, *stores]:
         store.wait()
 
 
@@ -517,12 +526,16 @@
             jax.ShapeDtypeStruct((BAND_ROWS, fields * levels), f32),
             jax.ShapeDtypeStruct((BAND_ROWS, levels), f32),
         ),
-        in_specs=[hbm, vmem],
-        out_specs=(hbm, vmem, vmem),
+        in_specs=[hbm, hbm],
+        out_specs=(hbm, hbm, hbm),
         scratch_shapes=[
             pltpu.VMEM((HANDED, 1, fields * levels * cols // HANDED, width), f32),
+            pltpu.VMEM((BAND_ROWS, LANES), f32),
+            pltpu.VMEM((BAND_ROWS, fields * levels), f32),
+            pltpu.VMEM((BAND_ROWS, levels), f32),
             dma((HANDED,)),
             dma((HANDED,)),
+            dma((3,)),
         ],
         compiler_params=pltpu.CompilerParams(vmem_limit_bytes=57 * 2**20),
     )(new_fields, means)

time: 51.5 us -> 49.8 us (0.967)
  Pallas kernels: 50.7 us -> 48.8 us
    pallas_call x1, Pallas kernels: 5.63 us -> 4.55 us  [on_device(): pl.pallas_call(hand_over, out_shape=(jax.ShapeDtypeStruct(merged, f32), j...]
    pallas_call x1, Pallas kernels: 45 us -> 44.3 us  [on_device(): pl.pallas_call(body, out_shape=(jax.ShapeDtypeStruct(merged, f32), jax.Sh...]
where the time goes in v3:
time: 49.8 us; the launch traced here: 49.5 us
  Pallas kernels  48.8 us (98%)
  between operations  0.64 us (1%)
    pallas_call x1, Pallas kernels, on_device(): pl.pallas_call(body, out_shape=(jax.ShapeDtypeStruct(merged, f32), jax.Sh...  44.3 us
    pallas_call x1, Pallas kernels, on_device(): pl.pallas_call(hand_over, out_shape=(jax.ShapeDtypeStruct(merged, f32), j...  4.55 us

profile of v3, /device:TPU:2, one launch (start us, length us, event | category | flops | bytes accessed | tf_op | source)
XLA Modules:
  0.0 49.5 jit_solution(13725139444981271097)
XLA Ops:
  0.6 44.3 %shard_map.103 = (f32[4,384,768]{2,1,0:T(8,128)}, f32[4,128]{1,0:T(4,128)}) custom-call(f32[16]{0:T(128)} %refs_0_.1, s32[4]{0:T(128)} %refs_1_.1, f32[16]{0:T(128)} %refs_2_.1, s32[128]{0:T(128)} %bitcast.10, f32[4,384,768]{2,1,0:T(8,128)} %bitcast.6, s32[128,128]{1,0:T(8,128)} %bitcast.7, s32[128,128]{1,0:T(8,128)} %bitcast.8, f32[128,128]{1,0:T(8,128)} %bitcast.9), custom_call_target="tpu_custom_call" | custom-call | tf_op jit(solution)/shard_map/pallas_call | solution.py:470
  44.9 4.5 %shard_map.104 = (f32[4,384,768]{2,1,0:T(8,128)}, f32[4,64]{1,0:T(4,128)}, f32[4,16]{1,0:T(4,128)}) custom-call(f32[4,384,768]{2,1,0:T(8,128)} %get-tuple-element.8.fields_in, f32[4,128]{1,0:T(4,128)} %get-tuple-element.9.means_in), custom_call_target="tpu_custom_call" | custom-call | tf_op jit(solution)/shard_map/pallas_call | solution.py:522

commit v4 on v3

--- a/solution.py
+++ b/solution.py
@@ -11,7 +11,7 @@
 GROUP = 8
 LANES = 128
 GATHERED = 8
-HANDED = 16
+HANDED = 4
 SCALE = 10.0**-SUBSTEPS
 
 f32 = jnp.float32
@@ -125,12 +125,15 @@
     def lanes_of(ref, j):
         return ref.at[:, :, pl.ds(j * LANES, LANES)]
 
-    loads = [
-        pltpu.make_async_copy(lanes_of(state, j), slab.at[:, j], load_sem.at[j])
-        for j in range(repeat)
-    ]
-    for load in loads:
-        load.start()
+    def load(g, j):
+        half = pl.ds(g * GROUP * cols, GROUP * cols)
+        return pltpu.make_async_copy(
+            state.at[:, half, pl.ds(j * LANES, LANES)], slab.at[:, j, half], load_sem.at[g, j]
+        )
+
+    for g in range(groups):
+        for j in range(repeat):
+            load(g, j).start()
     row_load = pltpu.make_async_copy(row, rows, row_sem)
     row_load.start()
     weight_load = pltpu.make_async_copy(weight, weights, weight_sem)
@@ -177,16 +180,17 @@
                 lifted = 0.5 * lifted if c == 2 else lifted
                 first[g, x + halo, c, :, pl.ds(j * LANES, LANES)] = lifted
 
-    for load in loads:
-        load.wait()
-
-    def lift_edge(i, carry):
-        g, j = lax.div(i, 2 * halo), lax.rem(i, 2 * halo)
-        lift(g, j + (cols - 2 * halo) * lax.div(j, halo))
-        return carry
-
-    lax.fori_loop(0, groups * 2 * halo, lift_edge, 0)
-
+    def lift_edges(g):
+        for j in range(repeat):
+            load(g, j).wait()
+
+        def lift_edge(i, carry):
+            lift(g, i + (cols - 2 * halo) * lax.div(i, halo))
+            return carry
+
+        lax.fori_loop(0, 2 * halo, lift_edge, 0)
+
+    lift_edges(0)
     pl.semaphore_wait(barrier, len(greeted))
 
     messages = [(g, 1, halo) for g in range(groups - 1)]
@@ -209,6 +213,9 @@
         )
 
     for m in range(len(messages)):
+        g = messages[m][0]
+        if m > 0 and g != messages[m - 1][0]:
+            lift_edges(g)
         for side in range(2):
             halo_copy(side, m).start()
     tell(0)
@@ -366,16 +373,13 @@
             spot_copy(turn, slot).wait()
             pick(slot)
             add_up(turn - 1, 1 - slot)
-
-            @pl.when(turn + 2 < rounds)
-            def _():
-                spot_copy(turn + 2, slot).start()
-
+            spot_copy(turn + 2, slot).start()
             send(turn - 1)
         return carry
 
     lax.fori_loop(0, rounds // 2 - 1, two_rounds, 0)
     spot_copy(rounds - 1, 1).wait()
+    spot_copy(rounds, 0).wait()
     pick(1)
     add_up(rounds - 2, 0)
     send(rounds - 2)
@@ -494,7 +498,7 @@
             pltpu.SMEM((n_face,), jnp.int32),
             pltpu.SMEM((levels,), f32),
             pltpu.SMEM((devices,), jnp.int32),
-            dma((width // LANES,)),
+            dma((groups, width // LANES)),
             dma,
             dma,
             dma((4,)),

time: 49.8 us -> 49.3 us (0.990)
  Pallas kernels: 48.8 us -> 48 us
where the time goes in v4:
time: 49.3 us; the launch traced here: 48.6 us
  Pallas kernels  48 us (97%)
  between operations  0.64 us (1%)
    pallas_call x1, Pallas kernels, on_device(): pl.pallas_call(body, out_shape=(jax.ShapeDtypeStruct(merged, f32), jax.Sh...  43.9 us
    pallas_call x1, Pallas kernels, on_device(): pl.pallas_call(hand_over, out_shape=(jax.ShapeDtypeStruct(merged, f32), j...  4.08 us

profile of v4, /device:TPU:2, one launch (start us, length us, event | category | flops | bytes accessed | tf_op | source)
XLA Modules:
  0.0 48.6 jit_solution(14482936955897850888)
XLA Ops:
  0.6 43.9 %shard_map.103 = (f32[4,384,768]{2,1,0:T(8,128)}, f32[4,128]{1,0:T(4,128)}) custom-call(f32[16]{0:T(128)} %refs_0_.1, s32[4]{0:T(128)} %refs_1_.1, f32[16]{0:T(128)} %refs_2_.1, s32[128]{0:T(128)} %bitcast.10, f32[4,384,768]{2,1,0:T(8,128)} %bitcast.6, s32[128,128]{1,0:T(8,128)} %bitcast.7, s32[128,128]{1,0:T(8,128)} %bitcast.8, f32[128,128]{1,0:T(8,128)} %bitcast.9), custom_call_target="tpu_custom_call" | custom-call | tf_op jit(solution)/shard_map/pallas_call | solution.py:474
  44.5 4.1 %shard_map.104 = (f32[4,384,768]{2,1,0:T(8,128)}, f32[4,64]{1,0:T(4,128)}, f32[4,16]{1,0:T(4,128)}) custom-call(f32[4,384,768]{2,1,0:T(8,128)} %get-tuple-element.8.fields_in, f32[4,128]{1,0:T(4,128)} %get-tuple-element.9.means_in), custom_call_target="tpu_custom_call" | custom-call | tf_op jit(solution)/shard_map/pallas_call | solution.py:526

commit v5 on v4

--- a/solution.py
+++ b/solution.py
@@ -398,8 +398,15 @@
     total_rows = BAND_ROWS * devices
     phi = ((lat_row.astype(f32) + 0.5) / total_rows - 0.5) * (jnp.pi / 2)
     cosine = jnp.cos(phi)
+    for m in range(len(messages)):
+        for side in range(2):
+            halo_copy(side, m).wait_send()
+    others.wait_send()
+    for store in stores:
+        store.wait()
     others.wait_recv()
-    total = jnp.sum(inbox[...], axis=0)
+    chains = inbox[...].reshape(devices // GATHERED, GATHERED, BAND_ROWS, LANES)
+    total = jnp.sum(jnp.sum(chains, axis=0), axis=0)
     ones_at = (FIELDS + 1) * levels
     means = total / jnp.broadcast_to(total[:, ones_at : ones_at + 1], total.shape)
     zonal = means
@@ -410,13 +417,6 @@
         k *= 2
     stream = cosine * means
     means_out[...] = jnp.where(lane < FIELDS * levels, zonal, stream)
-
-    for m in range(len(messages)):
-        for side in range(2):
-            halo_copy(side, m).wait_send()
-    others.wait_send()
-    for store in stores:
-        store.wait()
 
 
 def hand_over(

time: 49.3 us -> 49.2 us (level)
  no operation moved by 1% of the time
where the time goes in v5:
time: 49.2 us; the launch traced here: 48.5 us
  Pallas kernels  47.9 us (97%)
  between operations  0.64 us (1%)
    pallas_call x1, Pallas kernels, on_device(): pl.pallas_call(body, out_shape=(jax.ShapeDtypeStruct(merged, f32), jax.Sh...  43.8 us
    pallas_call x1, Pallas kernels, on_device(): pl.pallas_call(hand_over, out_shape=(jax.ShapeDtypeStruct(merged, f32), j...  4.08 us

profile of v5, /device:TPU:2, one launch (start us, length us, event | category | flops | bytes accessed | tf_op | source)
XLA Modules:
  0.0 48.5 jit_solution(10763419769380454377)
XLA Ops:
  0.6 43.8 %shard_map.103 = (f32[4,384,768]{2,1,0:T(8,128)}, f32[4,128]{1,0:T(4,128)}) custom-call(f32[16]{0:T(128)} %refs_0_.1, s32[4]{0:T(128)} %refs_1_.1, f32[16]{0:T(128)} %refs_2_.1, s32[128]{0:T(128)} %bitcast.10, f32[4,384,768]{2,1,0:T(8,128)} %bitcast.6, s32[128,128]{1,0:T(8,128)} %bitcast.7, s32[128,128]{1,0:T(8,128)} %bitcast.8, f32[128,128]{1,0:T(8,128)} %bitcast.9), custom_call_target="tpu_custom_call" | custom-call | tf_op jit(solution)/shard_map/pallas_call | solution.py:474
  44.4 4.1 %shard_map.104 = (f32[4,384,768]{2,1,0:T(8,128)}, f32[4,64]{1,0:T(4,128)}, f32[4,16]{1,0:T(4,128)}) custom-call(f32[4,384,768]{2,1,0:T(8,128)} %get-tuple-element.8.fields_in, f32[4,128]{1,0:T(4,128)} %get-tuple-element.9.means_in), custom_call_target="tpu_custom_call" | custom-call | tf_op jit(solution)/shard_map/pallas_call | solution.py:526
